TPU v7x, 32 devices: a whole 2x2x4 slice. The times are simulated.
32 devices in a mesh: parts: 2 (over x), gx: 16 (over z, y, core).
Axes of the slice: x: 2, y: 2, z: 4, core: 2. Of those that a mesh axis runs over, the one named last changes fastest.
Arguments:
- state: float32 [64, 512, 128], P(None, ('parts', 'gx')), parts along dimension 1, may hold values from -6 to 6
- cotangent: float32 [64, 512, 128], P(None, ('parts', 'gx')), parts along dimension 1, may hold values from -5 to 5
- kappa: float32 [512, 128], P(('parts', 'gx')), parts along dimension 0, may hold values from 0.04 to 0.2
- labels: int32 [512, 128], P(('parts', 'gx')), parts along dimension 0, may hold values from 0 to 3
- drift: float32 [64], replicated, may hold values from -0.6 to 0.6
- w_in: bfloat16 [4, 256, 64], replicated, may hold values from -0.75 to 0.75
- b_in: float32 [4, 256], replicated, may hold values from -3 to 3
- w_mid: bfloat16 [4, 256, 256], replicated, may hold values from -0.375 to 0.375
- b_mid: float32 [4, 256], replicated, may hold values from -3 to 3
- w_out: bfloat16 [4, 64, 256], replicated, may hold values from -0.375 to 0.375
- b_out: float32 [4, 64], replicated, may hold values from -3 to 3
Outputs:
- state_grad: float32 [64, 512, 128], P(None, ('parts', 'gx')), parts along dimension 1
- w_in_grad: float32 [8, 256, 64], P('parts'), parts along dimension 0
- b_in_grad: float32 [8, 256], P('parts'), parts along dimension 0
- w_mid_grad: float32 [8, 256, 256], P('parts'), parts along dimension 0
- b_mid_grad: float32 [8, 256], P('parts'), parts along dimension 0
- w_out_grad: float32 [8, 64, 256], P('parts'), parts along dimension 0
- b_out_grad: float32 [8, 64], P('parts'), parts along dimension 0
There are 2 independent parts, one for each index of `parts`. A program takes and returns all parts, laid end to end along the dimension named above; an argument that names none is the same for every part. Nothing has to cross between parts.
All inputs are finite; a program needn't handle non-finite values.
Results may differ from a plain program's by a relative error of at most 0.011.
Values sent between devices are 32-bit elements; how exact they have to be, the bound alone decides.
A program may use at most 128 MiB of HBM per device.

v0:
```python
import jax
import jax.numpy as jnp
from jax import lax
from jax.sharding import PartitionSpec as P

step_size = 0.8
gelu_coef = 0.7978845608028654


def with_halo(cells, sides, width):
    for axis, dim in sides:
        count = lax.axis_size(axis)
        head = lax.slice_in_dim(cells, 0, width, axis=dim)
        tail = lax.slice_in_dim(cells, cells.shape[dim] - width, cells.shape[dim], axis=dim)
        cells = jnp.concatenate(
            [
                lax.ppermute(tail, axis, [(i, (i + 1) % count) for i in range(count)]),
                cells,
                lax.ppermute(head, axis, [((i + 1) % count, i) for i in range(count)]),
            ],
            axis=dim,
        )
    return cells


def gelu_tanh(value):
    inner = gelu_coef * (value + 0.044715 * value * value * value)
    return 0.5 * value * (1.0 + jnp.tanh(inner))


def gelu_slope(value):
    inner = gelu_coef * (value + 0.044715 * value * value * value)
    tangent = jnp.tanh(inner)
    return 0.5 * (1.0 + tangent) + 0.5 * value * (1.0 - tangent * tangent) * gelu_coef * (
        1.0 + 3.0 * 0.044715 * value * value
    )


def expert_forward(columns, weights):
    w_in, b_in, w_mid, b_mid, w_out, b_out = weights
    col_bf = columns.astype(jnp.bfloat16)
    first = (
        jnp.einsum("ehk,kc->ehc", w_in, col_bf, preferred_element_type=jnp.float32)
        + b_in[:, :, None]
    )
    first_act = gelu_tanh(first).astype(jnp.bfloat16)
    second = (
        jnp.einsum("ehk,ekc->ehc", w_mid, first_act, preferred_element_type=jnp.float32)
        + b_mid[:, :, None]
    )
    second_act = gelu_tanh(second).astype(jnp.bfloat16)
    output = (
        jnp.einsum("ezk,ekc->ezc", w_out, second_act, preferred_element_type=jnp.float32)
        + b_out[:, :, None]
    )
    return (col_bf, first, first_act, second, second_act, output)


def expert_backward(projected, onehot, saved, weights):
    w_in, b_in, w_mid, b_mid, w_out, b_out = weights
    col_bf, first, first_act, second, second_act = saved
    cot_bf = projected.astype(jnp.bfloat16)
    masked = onehot.astype(jnp.bfloat16)[:, None, :] * cot_bf[None]
    d_out = jnp.einsum("ezc,ekc->ezk", masked, second_act, preferred_element_type=jnp.float32)
    db_out = jnp.sum(masked.astype(jnp.float32), axis=2)
    back_two = jnp.einsum(
        "ezk,ezc->ekc", w_out, masked, preferred_element_type=jnp.float32
    ) * gelu_slope(second)
    back_two_bf = back_two.astype(jnp.bfloat16)
    d_mid = jnp.einsum("ehc,ekc->ehk", back_two_bf, first_act, preferred_element_type=jnp.float32)
    db_mid = jnp.sum(back_two, axis=2)
    back_one = jnp.einsum(
        "ehk,ehc->ekc", w_mid, back_two_bf, preferred_element_type=jnp.float32
    ) * gelu_slope(first)
    back_one_bf = back_one.astype(jnp.bfloat16)
    d_in = jnp.einsum("ehc,kc->ehk", back_one_bf, col_bf, preferred_element_type=jnp.float32)
    db_in = jnp.sum(back_one, axis=2)
    col_grad = jnp.einsum("ehk,ehc->kc", w_in, back_one_bf, preferred_element_type=jnp.float32)
    return (col_grad, (d_in, db_in, d_mid, db_mid, d_out, db_out))


def forward_stencil(padded, kappa, drift):
    centre = padded[:, 1:-1]
    east = padded[:, 2:]
    west = padded[:, :-2]
    north = jnp.roll(centre, -1, axis=2)
    south = jnp.roll(centre, 1, axis=2)
    return (
        kappa[None] * (east + west + north + south - 4.0 * centre)
        - drift[:, None, None] * (east - west) * 0.5
    )


def adjoint_stencil(padded_pair, drift):
    cot_padded = padded_pair[0]
    weighted = padded_pair[1]
    centre = weighted[:, 1:-1]
    lap = (
        weighted[:, 2:]
        + weighted[:, :-2]
        + jnp.roll(centre, -1, axis=2)
        + jnp.roll(centre, 1, axis=2)
        - 4.0 * centre
    )
    return lap + drift[:, None, None] * (cot_padded[:, 2:] - cot_padded[:, :-2]) * 0.5


def shards(state, cotangent, kappa, labels, drift, w_in, b_in, w_mid, b_mid, w_out, b_out):
    weights = (w_in, b_in, w_mid, b_mid, w_out, b_out)
    levels, x_cells, y_cells = state.shape
    experts_here = w_in.shape[0]
    columns = x_cells * y_cells
    overall = columns * lax.axis_size("gx")
    regimes = jnp.arange(experts_here, dtype=jnp.int32)
    onehot = (
        (labels[None] == regimes[:, None, None]).astype(jnp.float32).reshape(experts_here, columns)
    )
    first_saved = expert_forward(state.reshape(levels, columns), weights)
    mix_first = jnp.sum(onehot[:, None, :] * first_saved[5], axis=0)
    scaled_late = 0.5 * step_size * cotangent
    stacked = jnp.stack([state, scaled_late, kappa[None] * scaled_late])
    rimmed = with_halo(stacked, (("gx", 2),), 1)
    mix_sum, late_sum = lax.psum(
        (jnp.sum(mix_first, axis=1), jnp.sum(scaled_late, axis=(1, 2))), "gx"
    )
    padded_state = rimmed[0]
    padded_late = rimmed[1:]
    closure_first = (mix_first - mix_sum[:, None] / overall).reshape(levels, x_cells, y_cells)
    section_field = state + step_size * (
        forward_stencil(padded_state, kappa, drift) + closure_first
    )
    second_saved = expert_forward(section_field.reshape(levels, columns), weights)
    late_proj = scaled_late.reshape(levels, columns) - late_sum[:, None] / overall
    late_cols, late_grads = expert_backward(late_proj, onehot, second_saved[:5], weights)
    mid_grad = (
        0.5 * cotangent
        + adjoint_stencil(padded_late, drift)
        + late_cols.reshape(levels, x_cells, y_cells)
    )
    late_grads = lax.psum(
        (late_grads[0], late_grads[1], late_grads[2], late_grads[3], late_grads[4], late_grads[5]),
        "gx",
    )
    scaled_early = step_size * mid_grad
    padded_early = with_halo(jnp.stack([scaled_early, kappa[None] * scaled_early]), (("gx", 2),), 1)
    early_sum = lax.psum(jnp.sum(scaled_early, axis=(1, 2)), "gx")
    early_proj = scaled_early.reshape(levels, columns) - early_sum[:, None] / overall
    early_cols, early_grads = expert_backward(early_proj, onehot, first_saved[:5], weights)
    state_grad = (
        0.5 * cotangent
        + mid_grad
        + adjoint_stencil(padded_early, drift)
        + early_cols.reshape(levels, x_cells, y_cells)
    )
    early_grads = lax.psum(
        (
            early_grads[0],
            early_grads[1],
            early_grads[2],
            early_grads[3],
            early_grads[4],
            early_grads[5],
        ),
        "gx",
    )
    summed = tuple((a + b for a, b in zip(late_grads, early_grads)))
    return (state_grad, summed[0], summed[1], summed[2], summed[3], summed[4], summed[5])


def solution(mesh):
    return jax.shard_map(
        shards,
        mesh=mesh,
        in_specs=(
            P(None, ("parts", "gx"), None),
            P(None, ("parts", "gx"), None),
            P(("parts", "gx"), None),
            P(("parts", "gx"), None),
            P(),
            P(),
            P(),
            P(),
            P(),
            P(),
            P(),
        ),
        out_specs=(
            P(None, ("parts", "gx"), None),
            P("parts", None, None),
            P("parts", None),
            P("parts", None, None),
            P("parts", None),
            P("parts", None, None),
            P("parts", None),
        ),
        check_vma=False,
    )
```

profile of v0, /device:TPU:0, one launch (start us, length us, event | category | flops | bytes accessed | tf_op | source)
XLA Modules:
  0.0 279.6 jit_solution(15815662364431644056)
XLA Ops:
  7.3 1.3 broadcast_multiply_fusion.2
  8.6 1.6 broadcast_multiply_fusion.1
  10.2 1.2 pad_maximum_fusion.4
  11.9 5.1 %collective-permute-start.1 = (f32[3,64,1,128]{3,2,1,0:T(1,128)S(1)}, f32[3,64,1,128]{3,2,1,0:T(1,128)}, u32[]{:S(2)}, u32[]{:S(2)}) collective-permute-start(f32[3,64,1,128]{3,2,1,0:T(1,128)S(1)} %get-tuple-element.27), channel_id=1, source_target_pairs={{1,0},{2,1},{3,2},{4,3},{5,4},{6,5},{7,6},{8,7},{9,8},{10,9},{11,1... | collective-permute-start | bytes 294920 | tf_op jit(solution)/shard_map/ppermute | solution.py:19
  16.9 1.1 convert_element_type.78
  18.0 0.7 fusion.93
  18.8 2.2 fusion.115
  21.1 7.6 %multiply_convert_fusion.2 = (bf16[4,256,2048]{1,2,0:T(8,128)(2,1)S(1)}, f32[4,2048,256]{2,1,0:T(8,128)}) fusion(f32[4,256]{1,0:T(4,128)S(1)} %copy-done.25, bf16[4,256,256]{2,1,0:T(8,128)(2,1)S(1)} %copy-done, f32[4,256,2048]{1,2,0:T(8,128)S(1)} %fusion.115, f32[4,256]{1,0:T(4,128)S(1)} %copy-done.27), kind=kOutput, calls=%fused_computation.37 | convolution fusion | flops 1115684864 | bytes 21504000 | tf_op jit(solution)/shard_map/ehk,ekc->ehc/dot_general | solution.py:48
  28.7 2.1 copy-done.4
  30.8 2.2 fusion.104
  33.0 30.3 %all-reduce.1 = (f32[64]{0:T(128)S(1)}, f32[64]{0:T(128)S(1)}) all-reduce(f32[64]{0:T(128)S(1)} %get-tuple-element.7, f32[64]{0:T(128)S(1)} %get-tuple-element.47), channel_id=1, replica_groups=mesh['parts'=2,'gx'=16] {'gx'}, use_global_device_ids=true, to_apply=%region_4.0 | all-reduce | flops 128 | bytes 1024 | tf_op jit(solution)/shard_map/psum | solution.py:123
  63.3 0.9 fusion.65
  64.2 1.1 copy.43
  65.4 1.2 pad_maximum_fusion
  66.7 1.0 slice_bitcast_fusion.4
  67.7 1.2 fusion.107
  68.9 1.1 fusion.108
  70.5 1.4 fusion.64
  71.9 1.1 reshape.118
  73.0 1.3 fusion.116
  74.3 3.5 %fusion.103 = f32[4,2048,256]{2,1,0:T(8,128)S(1)} fusion(bf16[4,256,256]{2,1,0:T(8,128)(2,1)S(1)} %copy-done, f32[2048,4,256]{2,0,1:T(8,128)S(1)} %fusion.116, f32[4,256]{1,0:T(4,128)S(1)} %copy-done.28), kind=kOutput, calls=%fused_computation.146 | convolution fusion | flops 1094713344 | bytes 17305600 | tf_op jit(solution)/shard_map/ehk,ekc->ehc/dot_general | solution.py:48
  77.8 3.8 %fusion.24 = f32[4,64,256]{2,1,0:T(8,128)} fusion(f32[4,2048,256]{2,1,0:T(8,128)S(1)} %fusion.103, f32[4,256]{1,0:T(4,128)S(1)} %copy-done.26, bf16[64,2048]{1,0:T(8,128)(2,1)S(1)} %copy-done.15, bf16[4,2048]{1,0:T(4,128)(2,1)S(1)} %get-tuple-element.51), kind=kOutput, calls=%fused_computation.39 | convolution fusion | flops 289931264 | bytes 8933376 | tf_op jit(solution)/shard_map/ezc,ekc->ezk/dot_general | solution.py:64
  81.6 7.3 %fusion.113 = (f32[4,256]{1,0:T(4,128)}, bf16[4,256,2048]{1,2,0:T(8,128)(2,1)S(1)}) fusion(f32[4,2048,256]{2,1,0:T(8,128)S(1)} %fusion.103, f32[4,256]{1,0:T(4,128)S(1)} %copy-done.26, bf16[4,64,256]{2,1,0:T(8,128)(2,1)S(1)} %copy-done.24, bf16[64,2048]{1,0:T(8,128)(2,1)S(1)} %copy-done.15, bf16[4,2048]{1,0:T(4,128)(2,1)S(1)} %get-tuple-element.51), kind=kOutput, calls=%fused_computation.156 | convolution fusion | flops 312998912 | bytes 13000704 | tf_op jit(solution)/shard_map/ezk,ezc->ekc/dot_general | solution.py:66
  89.0 6.8 %fusion.111 = (f32[4,256]{1,0:T(4,128)}, bf16[4,256,2048]{1,2,0:T(8,128)(2,1)S(1)}) fusion(f32[2048,4,256]{2,0,1:T(8,128)S(1)} %fusion.116, f32[4,256]{1,0:T(4,128)S(1)} %copy-done.28, bf16[4,256,256]{2,1,0:T(8,128)(2,1)S(1)} %copy-done, bf16[4,256,2048]{1,2,0:T(8,128)(2,1)S(1)} %get-tuple-element.60), kind=kOutput, calls=%fused_computation.154 | convolution fusion | flops 1117780992 | bytes 17309696 | tf_op jit(solution)/shard_map/ehk,ehc->ekc/dot_general | solution.py:72
  95.8 1.4 fusion.48
  98.0 1.1 multiply_bitcast_fusion
  99.2 29.5 %psum.107 = f32[64]{0:T(128)S(1)} all-reduce(f32[64]{0:T(128)S(1)} %get-tuple-element.43), channel_id=1, replica_groups=mesh['parts'=2,'gx'=16] {'gx'}, use_global_device_ids=true, to_apply=%region_6.7 | all-reduce | flops 64 | bytes 512 | tf_op jit(solution)/shard_map/psum | solution.py:146
  128.6 1.2 fusion.60
  129.9 9.3 %fusion.114 = (f32[4,256]{1,0:T(4,128)}, bf16[4,256,2048]{1,2,0:T(8,128)(2,1)S(1)}) fusion(f32[4,2048,256]{2,1,0:T(8,128)} %get-tuple-element.54, f32[4,256]{1,0:T(4,128)} %param.19, bf16[4,64,256]{2,1,0:T(8,128)(2,1)} %param.20, bf16[64,2048]{1,0:T(8,128)(2,1)S(1)} %fusion.60, bf16[4,2048]{1,0:T(4,128)(2,1)S(1)} %get-tuple-element.51), kind=kOutput, calls=%fused_computation.157 | convolution fusion | flops 312998912 | bytes 13000704 | tf_op jit(solution)/shard_map/ezk,ezc->ekc/dot_general | solution.py:66
  139.2 6.3 %fusion.30 = f32[4,256,256]{2,1,0:T(8,128)S(1)} fusion(bf16[4,256,2048]{1,2,0:T(8,128)(2,1)S(1)} %get-tuple-element.62, f32[4,256,2048]{1,2,0:T(8,128)} %copy-done.6, f32[4,256]{1,0:T(4,128)S(1)} %copy-done.29), kind=kOutput, calls=%fused_computation.49 | convolution fusion | flops 1094713344 | bytes 13635584 | tf_op jit(solution)/shard_map/ehc,ekc->ehk/dot_general | solution.py:70
  145.4 8.8 %fusion.112 = (f32[4,256]{1,0:T(4,128)}, bf16[4,256,2048]{1,2,0:T(8,128)(2,1)S(1)}) fusion(f32[4,256,2048]{1,2,0:T(8,128)} %copy-done.6, f32[4,256]{1,0:T(4,128)S(1)} %copy-done.29, bf16[4,256,256]{2,1,0:T(8,128)(2,1)S(1)} %copy-done, bf16[4,256,2048]{1,2,0:T(8,128)(2,1)S(1)} %get-tuple-element.62), kind=kOutput, calls=%fused_computation.155 | convolution fusion | flops 1117780992 | bytes 17309696 | tf_op jit(solution)/shard_map/ehk,ehc->ekc/dot_general | solution.py:72
  154.3 0.8 fusion.26
  155.1 2.2 fusion.51
  157.3 1.6 fusion.54
  158.8 0.7 pad_maximum_fusion.6
  159.6 4.4 %collective-permute-start.3 = (f32[2,64,1,128]{3,2,1,0:T(1,128)}, f32[2,64,1,128]{3,2,1,0:T(1,128)}, u32[]{:S(2)}, u32[]{:S(2)}) collective-permute-start(f32[2,64,1,128]{3,2,1,0:T(1,128)} %get-tuple-element.29), channel_id=1, source_target_pairs={{1,0},{2,1},{3,2},{4,3},{5,4},{6,5},{7,6},{8,7},{9,8},{10,9},{11,1... | collective-permute-start | bytes 196616 | tf_op jit(solution)/shard_map/ppermute | solution.py:19
  164.0 5.2 %fusion.45 = f32[4,256,256]{2,1,0:T(8,128)} fusion(f32[4,256,256]{2,1,0:T(8,128)S(1)} %fusion.30, bf16[4,256,2048]{1,2,0:T(8,128)(2,1)S(1)} %copy-done.32, f32[2048,4,256]{2,0,1:T(8,128)S(1)} %bitcast.130, f32[4,256]{1,0:T(4,128)S(1)} %copy-done.29), kind=kOutput, calls=%fused_computation.65 | convolution fusion | flops 1094975488 | bytes 14684160 | tf_op jit(solution)/shard_map/ehc,ekc->ehk/dot_general | solution.py:70
  169.2 1.5 fusion.57
  171.1 1.1 copy.46
  172.3 0.7 add.255
  173.0 0.7 add.253
  173.7 58.1 %all-reduce = (f32[4,256]{1,0:T(4,128)}, f32[4,256]{1,0:T(4,128)}, f32[4,64]{1,0:T(4,128)}) all-reduce(f32[4,256]{1,0:T(4,128)S(1)} %add.253, f32[4,256]{1,0:T(4,128)S(1)} %add.255, f32[4,64]{1,0:T(4,128)S(1)} %add.257), channel_id=1, replica_groups=mesh['parts'=2,'gx'=16] {'gx'}, use_global_device_ids=true, to_apply=%region_10.11 | all-reduce | flops 2304 | bytes 18432 | tf_op jit(solution)/shard_map/psum | solution.py:140
  231.7 1.1 pad_maximum_fusion.1
  233.4 1.4 bitcast_add_fusion
  234.8 32.4 %all-reduce.5.cloned.1.call-done = (f32[4,256,64]{1,2,0:T(8,128)}, f32[4,256,256]{2,1,0:T(8,128)}, f32[4,64,256]{2,1,0:T(8,128)}) async-done(((f32[4,256,64]{1,2,0:T(8,128)}, f32[4,256,256]{2,1,0:T(8,128)}, f32[4,64,256]{2,1,0:T(8,128)}), (f32[4,256,64]{1,2,0:T(8,128)}, f32[4,256,256]{2,1,0:T(8,128)}, f32[4,64,256]{2,1,0:T(8,128)})) %all-reduce.5.cloned.1.call-update) | async-done | bytes 1572880 | tf_op jit(solution)/shard_map/psum | solution.py:140
  267.1 1.7 copy.52
  268.8 2.3 copy.53
  271.1 1.7 copy.54
  (90 shorter events, 2.9 us)
Async XLA Ops:
  7.2 13.9 %copy-start = (bf16[4,256,256]{2,1,0:T(8,128)(2,1)S(1)}, bf16[4,256,256]{2,1,0:T(8,128)(2,1)}, u32[]{:S(2)}) copy-start(bf16[4,256,256]{2,1,0:T(8,128)(2,1)} %param.18) | copy-start | bytes 1572868
  7.2 13.9 %copy-start.27 = (f32[4,256]{1,0:T(4,128)S(1)}, f32[4,256]{1,0:T(4,128)}, u32[]{:S(2)}) copy-start(f32[4,256]{1,0:T(4,128)} %param.17) | copy-start | bytes 12292
  7.2 13.9 %copy-start.25 = (f32[4,256]{1,0:T(4,128)S(1)}, f32[4,256]{1,0:T(4,128)}, u32[]{:S(2)}) copy-start(f32[4,256]{1,0:T(4,128)} %param.19) | copy-start | bytes 12292
  7.2 259.9 %all-reduce.5.cloned.1.call-start = ((), (), s32[]{:S(2)}) async-start(), calls=%async_computation | async-start | bytes 3145728 | tf_op jit(solution)/shard_map/psum | solution.py:140
  11.3 54.0 %collective-permute-start = (f32[3,64,1,128]{3,2,1,0:T(1,128)S(1)}, f32[3,64,1,128]{3,2,1,0:T(1,128)S(1)}, u32[]{:S(2)}, u32[]{:S(2)}) collective-permute-start(f32[3,64,1,128]{3,2,1,0:T(1,128)S(1)} %get-tuple-element.26), channel_id=1, source_target_pairs={{0,1},{1,2},{2,3},{3,4},{4,5},{5,6},{6,7},{7,8},{8,9},{9,10},{10,1... | collective-permute-start | bytes 294920 | tf_op jit(solution)/shard_map/ppermute | solution.py:17
  11.9 53.5 %collective-permute-start.1 = (f32[3,64,1,128]{3,2,1,0:T(1,128)S(1)}, f32[3,64,1,128]{3,2,1,0:T(1,128)}, u32[]{:S(2)}, u32[]{:S(2)}) collective-permute-start(f32[3,64,1,128]{3,2,1,0:T(1,128)S(1)} %get-tuple-element.27), channel_id=1, source_target_pairs={{1,0},{2,1},{3,2},{4,3},{5,4},{6,5},{7,6},{8,7},{9,8},{10,9},{11,1... | collective-permute-start | bytes 294920 | tf_op jit(solution)/shard_map/ppermute | solution.py:19
  21.1 7.7 %copy-start.6 = (f32[4,256,2048]{1,2,0:T(8,128)}, f32[4,256,2048]{1,2,0:T(8,128)S(1)}, u32[]{:S(2)}) copy-start(f32[4,256,2048]{1,2,0:T(8,128)S(1)} %fusion.115) | copy-start | bytes 25165828
  21.1 9.7 %copy-start.23 = (bf16[4,64,256]{2,1,0:T(8,128)(2,1)S(1)}, bf16[4,64,256]{2,1,0:T(8,128)(2,1)}, u32[]{:S(2)}) copy-start(bf16[4,64,256]{2,1,0:T(8,128)(2,1)} %param.20) | copy-start | bytes 393220
  21.1 9.7 %copy-start.30 = (f32[4,64]{1,0:T(4,128)S(1)}, f32[4,64]{1,0:T(4,128)}, u32[]{:S(2)}) copy-start(f32[4,64]{1,0:T(4,128)} %param.21) | copy-start | bytes 3076
  21.1 44.3 %copy-start.7 = (f32[64,16,128]{2,1,0:T(8,128)S(1)}, f32[64,16,128]{2,1,0:T(8,128)}, u32[]{:S(2)}) copy-start(f32[64,16,128]{2,1,0:T(8,128)} %param.11) | copy-start | bytes 1572868
  28.7 2.1 copy-start.4
  65.4 5.1 %copy-start.18 = (f32[16,128]{1,0:T(8,128)S(1)}, f32[16,128]{1,0:T(8,128)}, u32[]{:S(2)}) copy-start(f32[16,128]{1,0:T(8,128)} %param.13) | copy-start | bytes 24580
  65.4 5.1 %copy-start.20 = (f32[64]{0:T(128)S(1)}, f32[64]{0:T(128)}, u32[]{:S(2)}) copy-start(f32[64]{0:T(128)} %param.15) | copy-start | bytes 772
  66.7 6.3 %copy-start.10 = (bf16[4,256,64]{1,2,0:T(8,128)(2,1)S(1)}, bf16[4,256,64]{1,2,0:T(8,128)(2,1)}, u32[]{:S(2)}) copy-start(bf16[4,256,64]{1,2,0:T(8,128)(2,1)} %param.16) | copy-start | bytes 393220
  71.9 2.4 copy-start.28
  74.3 14.7 %copy-start.3 = (f32[2048,4,256]{2,0,1:T(8,128)}, f32[2048,4,256]{2,0,1:T(8,128)S(1)}, u32[]{:S(2)}) copy-start(f32[2048,4,256]{2,0,1:T(8,128)S(1)} %fusion.116) | copy-start | bytes 25165828
  74.3 3.5 %copy-start.15 = (bf16[64,2048]{1,0:T(8,128)(2,1)S(1)}, bf16[64,2048]{1,0:T(8,128)(2,1)}, u32[]{:S(2)}) copy-start(bf16[64,2048]{1,0:T(8,128)(2,1)} %fusion.65) | copy-start | bytes 786436
  74.3 3.5 %copy-start.26 = (f32[4,256]{1,0:T(4,128)S(1)}, f32[4,256]{1,0:T(4,128)}, u32[]{:S(2)}) copy-start(f32[4,256]{1,0:T(4,128)} %param.19) | copy-start | bytes 12292
  77.8 3.8 %copy-start.24 = (bf16[4,64,256]{2,1,0:T(8,128)(2,1)S(1)}, bf16[4,64,256]{2,1,0:T(8,128)(2,1)}, u32[]{:S(2)}) copy-start(bf16[4,64,256]{2,1,0:T(8,128)(2,1)} %param.20) | copy-start | bytes 393220
  88.9 6.9 %copy-start.31 = (bf16[4,256,2048]{1,2,0:T(8,128)(2,1)}, bf16[4,256,2048]{1,2,0:T(8,128)(2,1)S(1)}, u32[]{:S(2)}) copy-start(bf16[4,256,2048]{1,2,0:T(8,128)(2,1)S(1)} %get-tuple-element.60) | copy-start | bytes 12582916
  88.9 8.4 %copy-start.8 = (f32[64,16,128]{2,1,0:T(8,128)S(1)}, f32[64,16,128]{2,1,0:T(8,128)}, u32[]{:S(2)}) copy-start(f32[64,16,128]{2,1,0:T(8,128)} %param.12) | copy-start | bytes 1572868
  88.9 8.4 %copy-start.9 = (f32[64,18,128]{2,1,0:T(8,128)S(1)}, f32[64,18,128]{2,1,0:T(8,128)}, u32[]{:S(2)}) copy-start(f32[64,18,128]{2,1,0:T(8,128)} %get-tuple-element.23) | copy-start | bytes 1769476
  88.9 8.4 %copy-start.11 = (f32[64,16,127]{2,1,0:T(8,128)S(1)}, f32[64,16,127]{2,1,0:T(8,128)}, u32[]{:S(2)}) copy-start(f32[64,16,127]{2,1,0:T(8,128)} %get-tuple-element.34) | copy-start | bytes 1560580
  89.0 8.4 %copy-start.12 = (f32[64,16,127]{2,1,0:T(8,128)S(1)}, f32[64,16,127]{2,1,0:T(8,128)}, u32[]{:S(2)}) copy-start(f32[64,16,127]{2,1,0:T(8,128)} %get-tuple-element.35) | copy-start | bytes 1560580
  89.0 8.4 %copy-start.13 = (f32[64,16,1]{2,1,0:T(8,128)S(1)}, f32[64,16,1]{2,1,0:T(8,128)}, u32[]{:S(2)}) copy-start(f32[64,16,1]{2,1,0:T(8,128)} %get-tuple-element.36) | copy-start | bytes 12292
  89.0 8.4 %copy-start.14 = (f32[64,16,1]{2,1,0:T(8,128)S(1)}, f32[64,16,1]{2,1,0:T(8,128)}, u32[]{:S(2)}) copy-start(f32[64,16,1]{2,1,0:T(8,128)} %get-tuple-element.37) | copy-start | bytes 12292
  89.0 8.4 %copy-start.21 = (f32[64]{0:T(128)S(1)}, f32[64]{0:T(128)}, u32[]{:S(2)}) copy-start(f32[64]{0:T(128)} %param.15) | copy-start | bytes 772
  95.8 2.2 copy-start.1
  95.8 2.2 copy-start.19
  129.9 9.3 %copy-start.29 = (f32[4,256]{1,0:T(4,128)S(1)}, f32[4,256]{1,0:T(4,128)}, u32[]{:S(2)}) copy-start(f32[4,256]{1,0:T(4,128)} %param.17) | copy-start | bytes 12292
  154.3 3.0 %copy-start.5 = (bf16[4,256,2048]{1,2,0:T(8,128)(2,1)S(1)}, bf16[4,256,2048]{1,2,0:T(8,128)(2,1)}, u32[]{:S(2)}) copy-start(bf16[4,256,2048]{1,2,0:T(8,128)(2,1)} %copy-done.4) | copy-start | bytes 12582916
  154.3 3.0 %copy-start.17 = (f32[4,64,256]{2,1,0:T(8,128)S(1)}, f32[4,64,256]{2,1,0:T(8,128)}, u32[]{:S(2)}) copy-start(f32[4,64,256]{2,1,0:T(8,128)} %fusion.24) | copy-start | bytes 786436
  154.3 9.8 %slice-start = ((s8[8388608]{0:T(1024)(128)(4,1)}), s8[4194304]{0:T(1024)(128)(4,1)S(1)}, s32[]{:S(2)}) async-start(s8[8388608]{0:T(1024)(128)(4,1)} %bitcast.129), calls=%async_computation.1 | async-start | bytes 8388608
  155.1 8.9 %slice-start.1 = ((s8[8388608]{0:T(1024)(128)(4,1)}), s8[4194304]{0:T(1024)(128)(4,1)S(1)}, s32[]{:S(2)}) async-start(s8[8388608]{0:T(1024)(128)(4,1)} %bitcast.129), calls=%async_computation.2 | async-start | bytes 8388608
  155.1 8.9 %copy-start.32 = (bf16[4,256,2048]{1,2,0:T(8,128)(2,1)S(1)}, bf16[4,256,2048]{1,2,0:T(8,128)(2,1)}, u32[]{:S(2)}) copy-start(bf16[4,256,2048]{1,2,0:T(8,128)(2,1)} %copy-done.31) | copy-start | bytes 12582916
  159.6 72.2 %collective-permute-start.2 = (f32[2,64,1,128]{3,2,1,0:T(1,128)}, f32[2,64,1,128]{3,2,1,0:T(1,128)}, u32[]{:S(2)}, u32[]{:S(2)}) collective-permute-start(f32[2,64,1,128]{3,2,1,0:T(1,128)} %get-tuple-element.28), channel_id=1, source_target_pairs={{0,1},{1,2},{2,3},{3,4},{4,5},{5,6},{6,7},{7,8},{8,9},{9,10},{10,1... | collective-permute-start | bytes 196616 | tf_op jit(solution)/shard_map/ppermute | solution.py:17
  159.6 9.6 %copy-start.2 = (bf16[4,256,2048]{1,2,0:T(8,128)(2,1)S(1)}, bf16[4,256,2048]{1,2,0:T(8,128)(2,1)}, u32[]{:S(2)}) copy-start(bf16[4,256,2048]{1,2,0:T(8,128)(2,1)} %copy-done.1) | copy-start | bytes 12582916
  159.6 11.1 %copy-start.16 = (bf16[64,2048]{1,0:T(8,128)(2,1)S(1)}, bf16[64,2048]{1,0:T(8,128)(2,1)}, u32[]{:S(2)}) copy-start(bf16[64,2048]{1,0:T(8,128)(2,1)} %fusion.65) | copy-start | bytes 786436
  159.6 72.2 %collective-permute-start.3 = (f32[2,64,1,128]{3,2,1,0:T(1,128)}, f32[2,64,1,128]{3,2,1,0:T(1,128)}, u32[]{:S(2)}, u32[]{:S(2)}) collective-permute-start(f32[2,64,1,128]{3,2,1,0:T(1,128)} %get-tuple-element.29), channel_id=1, source_target_pairs={{1,0},{2,1},{3,2},{4,3},{5,4},{6,5},{7,6},{8,7},{9,8},{10,9},{11,1... | collective-permute-start | bytes 196616 | tf_op jit(solution)/shard_map/ppermute | solution.py:19
  170.7 62.7 %copy-start.22 = (f32[64]{0:T(128)S(1)}, f32[64]{0:T(128)}, u32[]{:S(2)}) copy-start(f32[64]{0:T(128)} %param.15) | copy-start | bytes 772
Sparse Core Ops, SparseCore 0:
  173.8 93.2 all-reduce.4
where the time goes:
time: 280 us
  blocking collectives  118 us (42%)
  matrix products  71.7 us (26%)
  waiting for transfers between devices  32.4 us (12%)
  other arithmetic  17.4 us (6%)
  local copies, waits for them, and re-layouts  15.7 us (6%)
  between operations  14.5 us (5%)
  starting transfers between devices  10 us (4%)
    psum x1, blocking collectives, shards(): lax.psum((late_grads[0], late_grads[1], late_grads[2], late_grads[3], lat...  58.1 us
    psum x1, waiting for transfers between devices, shards(): lax.psum((late_grads[0], late_grads[1], late_grads[2], late_grads[3], lat...  32.4 us
    psum x1, blocking collectives, shards(): lax.psum((jnp.sum(mix_first, axis=1), jnp.sum(scaled_late, axis=(1, 2))),...  30.3 us
    psum x1, blocking collectives, shards(): early_sum = lax.psum(jnp.sum(scaled_early, axis=(1, 2)), 'gx')  29.5 us
    dot_general x2, matrix products, expert_backward(): jnp.einsum('ezk,ezc->ekc', w_out, masked, preferred_element_type=jnp.floa...  16.6 us
    dot_general x2, matrix products, expert_backward(): jnp.einsum('ehk,ehc->ekc', w_mid, back_two_bf, preferred_element_type=jnp...  15.6 us
    dot_general x2, matrix products, expert_backward(): jnp.einsum('ehc,ekc->ehk', back_two_bf, first_act, preferred_element_type...  11.4 us
    dot_general x2, matrix products, expert_forward(): jnp.einsum('ehk,ekc->ehc', w_mid, first_act, preferred_element_type=jnp.f...  11.1 us
  transfers between devices with their start and end apart: 5, of which 1 were waited for; matrix products, arithmetic and copies ran while one was open for 10% of the time, Pallas kernels for 0%

commit v1 on v0

v1 whole, which is shorter than its diff:
```python
import functools
import jax
import jax.numpy as jnp
from jax import lax
from jax.experimental import pallas as pl
from jax.experimental.pallas import tpu as pltpu
from jax.sharding import PartitionSpec as P

step_size = 0.8
gelu_coef = 0.7978845608028654
cubic = 0.044715
rows_per_chunk = 4
MESH = pl.DeviceIdType.MESH
f32, bf16 = jnp.float32, jnp.bfloat16


def dot(a, b):
    return jnp.dot(a, b, preferred_element_type=f32)


def dot_nt(a, b):
    return lax.dot_general(a, b, (((1,), (1,)), ((), ())), preferred_element_type=f32)


def gelu_pair(v):
    v2 = v * v
    t = jnp.tanh(v * (gelu_coef + (gelu_coef * cubic) * v2))
    h = 0.5 + 0.5 * t
    z = v * h
    slope = h + z * (1.0 - h) * (2.0 * gelu_coef + (6.0 * gelu_coef * cubic) * v2)
    return z.astype(bf16), slope


def to_row(col, at, nz):
    lane = lax.broadcasted_iota(jnp.int32, (nz, 128), 1)
    sub = lax.broadcasted_iota(jnp.int32, (nz, 128), 0)
    return jnp.sum(jnp.where(lane == sub + at, col, 0.0), axis=0, keepdims=True)


def to_col(row, at, nz):
    lane = lax.broadcasted_iota(jnp.int32, (nz, 128), 1)
    sub = lax.broadcasted_iota(jnp.int32, (nz, 128), 0)
    return jnp.sum(jnp.where(lane == sub + at, row, 0.0), axis=1, keepdims=True)


def main_kernel(
    n, state, cot, kappa, labels, drift, w_in, w_mid, w_out, bias,
    grad_out, sums_out,
    wi, wit, wm, wmt, wot, field, adj, mix, base, z1s, z2s, s1s, s2s, acc, mine, theirs,
    *rest,
):
    levels = rest[: len(rest) - 9]
    (halo_s, halo_r, halo2_s, halo2_r, sum_s, sum_r, red_s, red_r, whole) = rest[len(rest) - 9:]
    nz, nx, ny = state.shape
    ne, hid, _unused = w_in.shape
    nr = rows_per_chunk
    width = nr * ny
    chunks = nx // nr
    overall = nx * ny * n
    me = lax.axis_index("gx")
    right, left = lax.rem(me + 1, n), lax.rem(me + n - 1, n)
    r_in, r_mid, r_out = 0, hid, hid + ne * hid
    r_b = r_out + ne * nz

    barrier = pltpu.get_barrier_semaphore()
    for d in range(1, n):
        pl.semaphore_signal(barrier, inc=1, device_id={"gx": lax.rem(me + d, n)}, device_id_type=MESH)

    late_part = jnp.zeros((nz, ny), f32)
    for i in range(nx):
        c1 = (0.5 * step_size) * cot[:, i, :]
        late_part = late_part + c1
        field[i + 1, 0:nz] = state[:, i, :]
        field[i + 1, nz:2 * nz] = c1
        field[i + 1, 2 * nz:3 * nz] = kappa[i:i + 1, :] * c1
    pl.semaphore_wait(barrier, n - 1)

    def halo(ref, ss, rs):
        a = pltpu.make_async_remote_copy(
            src_ref=ref.at[nx], dst_ref=ref.at[0], send_sem=ss.at[0], recv_sem=rs.at[0],
            device_id={"gx": right}, device_id_type=MESH)
        b = pltpu.make_async_remote_copy(
            src_ref=ref.at[1], dst_ref=ref.at[nx + 1], send_sem=ss.at[1], recv_sem=rs.at[1],
            device_id={"gx": left}, device_id_type=MESH)
        a.start()
        b.start()
        return a, b

    first_halo = halo(field, halo_s, halo_r)

    wi[...] = jnp.concatenate([w_in[e] for e in range(ne)], axis=1)
    wit[...] = wi[...].T
    wm[...] = jnp.concatenate([w_mid[e] for e in range(ne)], axis=1)
    for e in range(ne):
        wmt[:, e * hid:(e + 1) * hid] = w_mid[e].T
    wot[...] = w_out[...].reshape(ne * nz, hid).T
    acc[...] = jnp.zeros_like(acc)

    def lab_of(c):
        return jnp.concatenate([labels[pl.ds(c * nr + r, 1), :] for r in range(nr)], axis=1)

    def pick(lab, parts):
        out = parts[ne - 1]
        for e in range(ne - 2, -1, -1):
            out = jnp.where(lab == e, parts[e], out)
        return out

    def masked(lab, val):
        m = val.shape[0]
        tiled = val.reshape(m // 16, 16, width)
        outs = []
        for e in range(ne):
            oh = jnp.broadcast_to(jnp.where(lab == e, 1.0, 0.0), (16, width)).astype(bf16)
            outs.append((tiled * oh[None]).reshape(m, width))
        return jnp.concatenate(outs, axis=0)

    def bias_of(lab, lo, size):
        return pick(lab, [bias[lo:lo + size, e:e + 1] for e in range(ne)])

    def forward(lab, q):
        hbm = masked(lab, q.astype(bf16))
        z1, s1 = gelu_pair(dot(wi[...], hbm) + bias_of(lab, 0, hid))
        z2, s2 = gelu_pair(dot(wm[...], masked(lab, z1)) + bias_of(lab, hid, hid))
        return hbm, z1, s1, z2, s2

    def add(row, val):
        rows = val.shape[0]
        acc[0, row:row + rows, :] += val[:, 0:128]
        acc[1, row:row + rows, :] += val[:, 128:256]

    def backward(lab, p, hbm, z1, s1, z2, s2):
        hot = jnp.where(lax.broadcasted_iota(jnp.int32, (16, width), 0) == lab, 1.0, 0.0).astype(bf16)
        gy = masked(lab, p.astype(bf16))
        add(r_out, dot_nt(gy, z2))
        add(r_b + 32, dot_nt(jnp.ones((16, width), bf16), gy))
        gab2 = (dot(wot[...], gy) * s2).astype(bf16)
        gab2m = masked(lab, gab2)
        add(r_mid, dot_nt(gab2m, z1))
        add(r_b + 16, dot_nt(hot, gab2))
        gab1 = (dot(wmt[...], gab2m) * s1).astype(bf16)
        add(r_in, dot_nt(gab1, hbm))
        add(r_b, dot_nt(hot, gab1))
        cols = dot(wit[...], gab1)
        return pick(lab, [cols[e * nz:(e + 1) * nz] for e in range(ne)])

    def rowcat(ref, c, lo):
        return jnp.concatenate([ref[c * nr + r + 1, lo:lo + nz] for r in range(nr)], axis=1)

    def first(c, part):
        lab = lab_of(c)
        _, z1, s1, z2, s2 = forward(lab, rowcat(field, c, 0))
        z1s[c], s1s[c], z2s[c], s2s[c] = z1, s1, z2, s2
        y = dot(w_out[...].reshape(ne * nz, hid), z2)
        m = pick(lab, [y[e * nz:(e + 1) * nz] for e in range(ne)]) + bias_of(lab, 2 * hid, nz)
        for r in range(nr):
            block = m[:, r * ny:(r + 1) * ny]
            mix[c * nr + r] = block
            part = part + block
        return part

    mix_part = lax.fori_loop(0, chunks, first, jnp.zeros((nz, ny), f32))

    def exchange(k, row):
        mine[k] = jnp.broadcast_to(row, (8, 128))
        copies = []
        for d in range(1, n):
            copies.append(pltpu.make_async_remote_copy(
                src_ref=mine.at[k], dst_ref=theirs.at[k, d], send_sem=sum_s.at[k, d],
                recv_sem=sum_r.at[k, d], device_id={"gx": lax.rem(me + d, n)}, device_id_type=MESH))
        for copy in copies:
            copy.start()
        return copies

    def collect(k, copies):
        total = mine[k]
        for d in range(1, n):
            copies[d - 1].wait()
            total = total + theirs[k, d]
        return total[0:1] * (1.0 / overall)

    sums = exchange(0, to_row(jnp.sum(mix_part, axis=1, keepdims=True), 0, nz)
                    + to_row(jnp.sum(late_part, axis=1, keepdims=True), nz, nz))
    for copy in first_halo:
        copy.wait()
    means = collect(0, sums)
    mix_mean, late_mean = to_col(means, 0, nz), to_col(means, nz, nz)
    speed = 0.5 * to_col(drift[...], 0, nz)

    def second(c, part):
        lab = lab_of(c)
        qs = []
        for r in range(nr):
            i = c * nr + r
            here, east, west = field[i + 1, 0:nz], field[i + 2, 0:nz], field[i, 0:nz]
            around = east + west + pltpu.roll(here, 127, 1) + pltpu.roll(here, 1, 1) - 4.0 * here
            lq = kappa[pl.ds(i, 1), :] * around - speed * (east - west)
            qs.append(here + step_size * (lq + mix[i] - mix_mean))
        hbm, z1, s1, z2, s2 = forward(lab, jnp.concatenate(qs, axis=1))
        p = rowcat(field, c, nz) - late_mean
        cols = backward(lab, p, hbm, z1, s1, z2, s2)
        for r in range(nr):
            i = c * nr + r
            half_cot = (0.5 / (0.5 * step_size)) * field[i + 1, nz:2 * nz]
            back = adjoint(field, i, nz, 2 * nz) + cols[:, r * ny:(r + 1) * ny]
            mid = half_cot + back
            c0 = step_size * mid
            base[i] = half_cot + mid
            adj[i + 1, 0:nz] = c0
            adj[i + 1, nz:2 * nz] = kappa[pl.ds(i, 1), :] * c0
            part = part + c0
        return part

    def adjoint(ref, i, c_at, k_at):
        k = ref[i + 1, k_at:k_at + nz]
        lap = (ref[i + 2, k_at:k_at + nz] + ref[i, k_at:k_at + nz]
               + pltpu.roll(k, 127, 1) + pltpu.roll(k, 1, 1) - 4.0 * k)
        return lap + speed * (ref[i + 2, c_at:c_at + nz] - ref[i, c_at:c_at + nz])

    early_part = lax.fori_loop(0, chunks, second, jnp.zeros((nz, ny), f32))
    sums = exchange(1, to_row(jnp.sum(early_part, axis=1, keepdims=True), 0, nz))
    second_halo = halo(adj, halo2_s, halo2_r)
    early_mean = to_col(collect(1, sums), 0, nz)
    for copy in second_halo:
        copy.wait()

    def third(c, carry):
        lab = lab_of(c)
        hbm = masked(lab, rowcat(field, c, 0).astype(bf16))
        p = rowcat(adj, c, 0) - early_mean
        cols = backward(lab, p, hbm, z1s[c], s1s[c], z2s[c], s2s[c])
        for r in range(nr):
            i = c * nr + r
            grad_out[i] = base[i] + adjoint(adj, i, 0, nz) + cols[:, r * ny:(r + 1) * ny]
        return carry

    lax.fori_loop(0, chunks, third, 0)

    bits = len(levels)
    orders = [list(range(bits)), [0] + list(range(2, bits)) + [1]]
    total = acc.shape[1]
    offs = [[jnp.int32(0)], [jnp.int32(0)]]

    def plan(s, t):
        b = orders[s][t]
        half = total >> (t + 1)
        bit = lax.rem(me // (1 << b), 2)
        off = offs[s][t]
        keep = pl.multiple_of(off + bit * half, 8)
        send = pl.multiple_of(off + (1 - bit) * half, 8)
        return half, keep, send, me + (1 - 2 * bit) * (1 << b)

    def start_reduce(s, t):
        half, keep, send, partner = plan(s, t)
        copy = pltpu.make_async_remote_copy(
            src_ref=acc.at[s, pl.ds(send, half)], dst_ref=levels[t].at[s], send_sem=red_s.at[s, t],
            recv_sem=red_r.at[s, t], device_id={"gx": partner}, device_id_type=MESH)
        copy.start()
        offs[s].append(keep)
        return copy, half, keep

    def start_gather(s, t):
        half, keep, _, partner = plan(s, t)
        copy = pltpu.make_async_remote_copy(
            src_ref=whole.at[s, pl.ds(keep, half)], dst_ref=whole.at[s, pl.ds(keep, half)],
            send_sem=red_s.at[s, bits + t], recv_sem=red_r.at[s, bits + t],
            device_id={"gx": partner}, device_id_type=MESH)
        copy.start()
        return copy

    flying = [start_reduce(s, 0) for s in range(2)]
    for t in range(bits):
        for s in range(2):
            copy, half, keep = flying[s]
            copy.wait()
            reduced = acc[s, pl.ds(keep, half), :] + levels[t][s]
            if t + 1 < bits:
                acc[s, pl.ds(keep, half), :] = reduced
                flying[s] = start_reduce(s, t + 1)
            else:
                whole[s, pl.ds(keep, half), :] = reduced
                flying[s] = start_gather(s, t)
    for t in range(bits - 1, -1, -1):
        for s in range(2):
            flying[s].wait()
            if t > 0:
                flying[s] = start_gather(s, t - 1)
    sums_out[...] = whole[...]


def output_kernel(grad, sums, state_grad, dw_in, db_in, dw_mid, db_mid, dw_out, db_out):
    ne, hid, nz = dw_in.shape
    r_mid, r_out = hid, hid + ne * hid
    r_b = r_out + ne * nz
    for i in range(grad.shape[0]):
        state_grad[:, i, :] = grad[i]
    per = 128 // nz
    for e in range(ne):
        s, at = e // per, (e % per) * nz
        dw_in[e] = sums[s, 0:hid, at:at + nz]
        db_out[e:e + 1, :] = sums[s, r_b + 32:r_b + 33, at:at + nz]
        for s in range(2):
            lanes = slice(s * 128, (s + 1) * 128)
            dw_mid[e, :, lanes] = sums[s, r_mid + e * hid:r_mid + (e + 1) * hid, :]
            dw_out[e, :, lanes] = sums[s, r_out + e * nz:r_out + (e + 1) * nz, :]
    for s in range(2):
        lanes = slice(s * 128, (s + 1) * 128)
        db_in[:, lanes] = sums[s, r_b:r_b + ne, :]
        db_mid[:, lanes] = sums[s, r_b + 16:r_b + 16 + ne, :]


def shards(state, cotangent, kappa, labels, drift, w_in, b_in, w_mid, b_mid, w_out, b_out):
    nz, nx, ny = state.shape
    ne, hid, _ = w_in.shape
    n = lax.axis_size("gx")
    bits = n.bit_length() - 1
    rows = hid + ne * hid + ne * nz + 8 * n
    bias = jnp.concatenate([b_in, b_mid, b_out], axis=1).T
    drift_row = jnp.pad(drift[None], ((0, 0), (0, 128 - nz)))
    chunks, width = nx // rows_per_chunk, rows_per_chunk * ny
    vmem = pl.BlockSpec(memory_space=pltpu.VMEM)
    sds = jax.ShapeDtypeStruct
    grad, sums = pl.pallas_call(
        functools.partial(main_kernel, n),
        out_shape=(sds((nx, nz, ny), f32), sds((2, rows, 128), f32)),
        in_specs=[vmem] * 9,
        out_specs=(vmem, vmem),
        scratch_shapes=[
            pltpu.VMEM((hid, ne * nz), bf16),
            pltpu.VMEM((ne * nz, hid), bf16),
            pltpu.VMEM((hid, ne * hid), bf16),
            pltpu.VMEM((hid, ne * hid), bf16),
            pltpu.VMEM((hid, ne * nz), bf16),
            pltpu.VMEM((nx + 2, 3 * nz, ny), f32),
            pltpu.VMEM((nx + 2, 2 * nz, ny), f32),
            pltpu.VMEM((nx, nz, ny), f32),
            pltpu.VMEM((nx, nz, ny), f32),
            pltpu.VMEM((chunks, hid, width), bf16),
            pltpu.VMEM((chunks, hid, width), bf16),
            pltpu.VMEM((chunks, hid, width), f32),
            pltpu.VMEM((chunks, hid, width), f32),
            pltpu.VMEM((2, rows, 128), f32),
            pltpu.VMEM((2, 8, 128), f32),
            pltpu.VMEM((2, n, 8, 128), f32),
        ]
        + [pltpu.VMEM((2, rows >> (t + 1), 128), f32) for t in range(bits)]
        + [
            pltpu.SemaphoreType.DMA((2,)),
            pltpu.SemaphoreType.DMA((2,)),
            pltpu.SemaphoreType.DMA((2,)),
            pltpu.SemaphoreType.DMA((2,)),
            pltpu.SemaphoreType.DMA((2, n)),
            pltpu.SemaphoreType.DMA((2, n)),
            pltpu.SemaphoreType.DMA((2, 2 * bits)),
            pltpu.SemaphoreType.DMA((2, 2 * bits)),
            pltpu.VMEM((2, rows, 128), f32),
        ],
        compiler_params=pltpu.CompilerParams(
            collective_id=0, has_side_effects=True, vmem_limit_bytes=48 * 1024 * 1024),
        name="heun_reverse",
    )(state, cotangent, kappa, labels, drift_row, w_in, w_mid, w_out, bias)
    return tuple(pl.pallas_call(
        output_kernel,
        out_shape=(
            sds((nz, nx, ny), f32), sds((ne, hid, nz), f32), sds((ne, hid), f32),
            sds((ne, hid, hid), f32), sds((ne, hid), f32), sds((ne, nz, hid), f32), sds((ne, nz), f32)),
        in_specs=[vmem] * 2,
        out_specs=(vmem,) * 7,
        compiler_params=pltpu.CompilerParams(vmem_limit_bytes=32 * 1024 * 1024),
        name="place_outputs",
    )(grad, sums))


def solution(mesh):
    cells, replicated = P(None, ("parts", "gx"), None), P()
    return jax.shard_map(
        shards,
        mesh=mesh,
        in_specs=(cells, cells, P(("parts", "gx"), None), P(("parts", "gx"), None)) + (replicated,) * 7,
        out_specs=(cells, P("parts", None, None), P("parts", None), P("parts", None, None),
                   P("parts", None), P("parts", None, None), P("parts", None)),
        check_vma=False,
    )
```

time: 280 us -> 85 us (0.30)
  blocking collectives: 118 us -> 0 us
  Pallas kernels: 0 us -> 75 us
  matrix products: 71.7 us -> 0 us
  waiting for transfers between devices: 32.4 us -> 0 us
  other arithmetic: 17.4 us -> 0.72 us
  between operations: 14.5 us -> 0.67 us
  starting transfers between devices: 10 us -> 0 us
  local copies, waits for them, and re-layouts: 15.7 us -> 8.2 us
    psum x3 -> x0, blocking collectives: 118 us -> none  [the longest x1 58.1 us: shards(): lax.psum((late_grads[0], late_grads[1], late_grads[2], late_grads[3], lat...]
    pallas_call x0 -> x2, Pallas kernels: none -> 75 us  [the longest x1 73.3 us: shards(): pl.pallas_call(functools.partial(main_kernel, n), out_shape=(sds((nx, nz,...]
    dot_general x17 -> x0, matrix products: 71.7 us -> none  [the longest x2 16.6 us: expert_backward(): jnp.einsum('ezk,ezc->ekc', w_out, masked, preferred_element_type=jnp.floa...]
    psum x1 -> x0, waiting for transfers between devices: 32.4 us -> none  [shards(): lax.psum((late_grads[0], late_grads[1], late_grads[2], late_grads[3], lat...]
    ppermute x4 -> x0, starting transfers between devices: 10 us -> none  [the longest x2 9.5 us: with_halo(): lax.ppermute(head, axis, [((i + 1) % count, i) for i in range(count)])]
    convert_element_type x5 -> x0, other arithmetic: 5.33 us -> none  [the longest x2 2.52 us: expert_forward(): col_bf = columns.astype(jnp.bfloat16)]
    unnamed x76 -> x13, local copies, waits for them, and re-layouts: 10.2 us -> 6.49 us
    slice x6 -> x0, local copies, waits for them, and re-layouts: 3.13 us -> none  [the longest x2 2.3 us: adjoint_stencil(): jnp.roll(centre, -1, axis=2)]
  transfers between devices with their start and end apart: 5 -> 0, of which waited for: 1 -> 0; matrix products, arithmetic and copies ran while one was open for 10% -> 0% of each run, Pallas kernels for 0% -> 0%
where the time goes in v1:
time: 85 us; the launch traced here: 84.6 us
  Pallas kernels  75 us (88%)
  local copies, waits for them, and re-layouts  8.2 us (10%)
    pallas_call x1, Pallas kernels, shards(): pl.pallas_call(functools.partial(main_kernel, n), out_shape=(sds((nx, nz,...  73.3 us
    unnamed x13, local copies, waits for them, and re-layouts  6.49 us

profile of v1, /device:TPU:0, one launch (start us, length us, event | category | flops | bytes accessed | tf_op | source)
XLA Modules:
  0.0 84.6 jit_solution(9603920116145939100)
XLA Ops:
  0.6 0.7 pad.4.drift
  1.3 0.7 pad_maximum_fusion
  2.0 1.1 %copy.24.w_in = bf16[4,256,64]{2,1,0:T(8,128)(2,1)S(1)} copy(bf16[4,256,64]{1,2,0:T(8,128)(2,1)} %param.16) | data formatting | bytes 262144 | tf_op args[5]
  3.1 0.2 copy.23
  3.3 0.0 copy-start
  3.3 1.0 %copy-done = f32[64,16,128]{2,1,0:T(8,128)S(1)} copy-done((f32[64,16,128]{2,1,0:T(8,128)S(1)}, f32[64,16,128]{2,1,0:T(8,128)}, u32[]{:S(2)}) %copy-start) | copy-done | bytes 524312
  4.3 0.0 copy-start.1
  4.3 1.0 %copy-done.1 = f32[64,16,128]{2,1,0:T(8,128)S(1)} copy-done((f32[64,16,128]{2,1,0:T(8,128)S(1)}, f32[64,16,128]{2,1,0:T(8,128)}, u32[]{:S(2)}) %copy-start.1) | copy-done | bytes 524312
  5.4 0.0 copy-start.2
  5.4 1.0 %copy-done.2 = bf16[4,256,256]{2,1,0:T(8,128)(2,1)S(1)} copy-done((bf16[4,256,256]{2,1,0:T(8,128)(2,1)S(1)}, bf16[4,256,256]{2,1,0:T(8,128)(2,1)}, u32[]{:S(2)}) %copy-start.2) | copy-done | bytes 524312
  6.4 0.0 copy-start.3
  6.4 0.9 %copy-done.3 = bf16[4,64,256]{2,1,0:T(8,128)(2,1)S(1)} copy-done((bf16[4,64,256]{2,1,0:T(8,128)(2,1)S(1)}, bf16[4,64,256]{2,1,0:T(8,128)(2,1)}, u32[]{:S(2)}) %copy-start.3) | copy-done | bytes 131096
  7.3 0.0 copy-start.4
  7.3 0.7 copy-done.4
  8.0 0.0 copy-start.5
  8.0 0.7 copy-done.5
  8.7 73.3 %heun_reverse.1 = (f32[16,64,128]{2,1,0:T(8,128)S(1)}, f32[2,1664,128]{2,1,0:T(8,128)S(1)}) custom-call(f32[64,16,128]{2,1,0:T(8,128)S(1)} %copy-done, f32[64,16,128]{2,1,0:T(8,128)S(1)} %copy-done.1, f32[16,128]{1,0:T(8,128)S(1)} %copy-done.4, s32[16,128]{1,0:T(8,128)S(1)} %copy-done.5, f32[1,128]{1,0:T(1,128)S(1)} %pad.4.drift, ...), custom_call_target="tpu_custom_call" | custom-call | tf_op jit(solution)/shard_map/heun_reverse/pallas_call | solution.py:322
  82.0 1.7 %place_outputs.1 = (f32[64,16,128]{2,1,0:T(8,128)}, f32[4,256,64]{2,1,0:T(8,128)S(1)}, f32[4,256]{1,0:T(4,128)}, f32[4,256,256]{2,1,0:T(8,128)}, f32[4,256]{1,0:...) custom-call(f32[16,64,128]{2,1,0:T(8,128)S(1)} %get-tuple-element.9.grad, f32[2,1664,128]{2,1,0:T(8,128)S(1)} %get-tuple-element.10.sums), custom_call_target="tpu_custom_call" | custom-call | tf_op jit(solution)/shard_map/place_outputs/pallas_call | solution.py:361
  83.7 0.9 %copy.25 = f32[4,256,64]{1,2,0:T(8,128)} copy(f32[4,256,64]{2,1,0:T(8,128)S(1)} %get-tuple-element.19) | data formatting | bytes 524288 | tf_op jit(solution)/shard_map/place_outputs/pallas_call | solution.py:361
Async XLA Ops:
  3.3 1.0 %copy-start = (f32[64,16,128]{2,1,0:T(8,128)S(1)}, f32[64,16,128]{2,1,0:T(8,128)}, u32[]{:S(2)}) copy-start(f32[64,16,128]{2,1,0:T(8,128)} %state.1) | copy-start | bytes 1572868
  4.3 1.0 %copy-start.1 = (f32[64,16,128]{2,1,0:T(8,128)S(1)}, f32[64,16,128]{2,1,0:T(8,128)}, u32[]{:S(2)}) copy-start(f32[64,16,128]{2,1,0:T(8,128)} %cot.1) | copy-start | bytes 1572868
  5.4 1.0 %copy-start.2 = (bf16[4,256,256]{2,1,0:T(8,128)(2,1)S(1)}, bf16[4,256,256]{2,1,0:T(8,128)(2,1)}, u32[]{:S(2)}) copy-start(bf16[4,256,256]{2,1,0:T(8,128)(2,1)} %w_mid.1) | copy-start | bytes 1572868
  6.4 0.9 %copy-start.3 = (bf16[4,64,256]{2,1,0:T(8,128)(2,1)S(1)}, bf16[4,64,256]{2,1,0:T(8,128)(2,1)}, u32[]{:S(2)}) copy-start(bf16[4,64,256]{2,1,0:T(8,128)(2,1)} %w_out.1) | copy-start | bytes 393220
  7.3 0.7 copy-start.4
  8.0 0.7 copy-start.5

commit v2 on v1

--- a/solution.py
+++ b/solution.py
@@ -9,7 +9,7 @@
 step_size = 0.8
 gelu_coef = 0.7978845608028654
 cubic = 0.044715
-rows_per_chunk = 4
+rows_per_chunk = 16
 MESH = pl.DeviceIdType.MESH
 f32, bf16 = jnp.float32, jnp.bfloat16
 
@@ -38,34 +38,42 @@
 
 
 def to_col(row, at, nz):
-    lane = lax.broadcasted_iota(jnp.int32, (nz, 128), 1)
-    sub = lax.broadcasted_iota(jnp.int32, (nz, 128), 0)
+    shape = (nz, row.shape[1])
+    lane = lax.broadcasted_iota(jnp.int32, shape, 1)
+    sub = lax.broadcasted_iota(jnp.int32, shape, 0)
     return jnp.sum(jnp.where(lane == sub + at, row, 0.0), axis=1, keepdims=True)
 
 
 def main_kernel(
-    n, state, cot, kappa, labels, drift, w_in, w_mid, w_out, bias,
+    n, state_h, cot_h, kappa_h, labels_h, drift_h, w_in_h, w_mid_h, w_out_h, b_in_h, b_mid_h, b_out_h,
     grad_out, sums_out,
+    state, cot, kappa, labels, drift, w_in, w_mid, w_out, b_in, b_mid, b_out, load, bias,
     wi, wit, wm, wmt, wot, field, adj, mix, base, z1s, z2s, s1s, s2s, acc, mine, theirs,
-    *rest,
+    inbox, halo_s, halo_r, halo2_s, halo2_r, sum_s, sum_r, red_s, red_r, whole,
 ):
-    levels = rest[: len(rest) - 9]
-    (halo_s, halo_r, halo2_s, halo2_r, sum_s, sum_r, red_s, red_r, whole) = rest[len(rest) - 9:]
     nz, nx, ny = state.shape
-    ne, hid, _unused = w_in.shape
+    ne, nz_in, hid = w_in.shape
     nr = rows_per_chunk
     width = nr * ny
     chunks = nx // nr
     overall = nx * ny * n
     me = lax.axis_index("gx")
     right, left = lax.rem(me + 1, n), lax.rem(me + n - 1, n)
-    r_in, r_mid, r_out = 0, hid, hid + ne * hid
+    r_in, r_mid, r_out = 0, ne * nz, ne * nz + ne * hid
     r_b = r_out + ne * nz
 
     barrier = pltpu.get_barrier_semaphore()
     for d in range(1, n):
         pl.semaphore_signal(barrier, inc=1, device_id={"gx": lax.rem(me + d, n)}, device_id_type=MESH)
 
+    pairs = [(state_h, state), (cot_h, cot), (kappa_h, kappa), (labels_h, labels), (drift_h, drift),
+             (w_in_h, w_in), (w_mid_h, w_mid), (w_out_h, w_out), (b_in_h, b_in), (b_mid_h, b_mid),
+             (b_out_h, b_out)]
+    loads = [pltpu.make_async_copy(src, dst, load.at[i]) for i, (src, dst) in enumerate(pairs)]
+    for i in (0, 1, 2, 5, 6, 7, 8, 9, 10, 3, 4):
+        loads[i].start()
+    for i in (0, 1, 2):
+        loads[i].wait()
     late_part = jnp.zeros((nz, ny), f32)
     for i in range(nx):
         c1 = (0.5 * step_size) * cot[:, i, :]
@@ -88,8 +96,15 @@
 
     first_halo = halo(field, halo_s, halo_r)
 
-    wi[...] = jnp.concatenate([w_in[e] for e in range(ne)], axis=1)
-    wit[...] = wi[...].T
+    for i in range(3, len(loads)):
+        loads[i].wait()
+    wit[...] = w_in[...].reshape(ne * nz, hid)
+    wi[...] = wit[...].T
+    at = 0
+    for b in (b_in, b_mid, b_out):
+        size = b.shape[1]
+        bias[at:at + size] = jnp.concatenate([b[...], jnp.zeros((8 - ne, size), f32)], axis=0).T
+        at += size
     wm[...] = jnp.concatenate([w_mid[e] for e in range(ne)], axis=1)
     for e in range(ne):
         wmt[:, e * hid:(e + 1) * hid] = w_mid[e].T
@@ -138,7 +153,7 @@
         add(r_mid, dot_nt(gab2m, z1))
         add(r_b + 16, dot_nt(hot, gab2))
         gab1 = (dot(wmt[...], gab2m) * s1).astype(bf16)
-        add(r_in, dot_nt(gab1, hbm))
+        add(r_in, dot_nt(hbm, gab1))
         add(r_b, dot_nt(hot, gab1))
         cols = dot(wit[...], gab1)
         return pick(lab, [cols[e * nz:(e + 1) * nz] for e in range(ne)])
@@ -235,71 +250,98 @@
 
     lax.fori_loop(0, chunks, third, 0)
 
-    bits = len(levels)
-    orders = [list(range(bits)), [0] + list(range(2, bits)) + [1]]
-    total = acc.shape[1]
-    offs = [[jnp.int32(0)], [jnp.int32(0)]]
+    bits = n.bit_length() - 1
+    units = acc.shape[1] // (8 * n)
+    low = (units // 2) * 8 * n
+    rest_bits = [list(range(b, b + 1)) for b in range(2, bits)]
+    near_first = [[0], [1]] + rest_bits
+    far_first = [[0]] + rest_bits + [[1]]
+    streams = [(0, 0, low, near_first), (1, 0, low, far_first),
+               (0, low, acc.shape[1] - low, far_first), (1, low, acc.shape[1] - low, near_first)]
+    stages = len(near_first)
+    digit = [lax.rem(me // (1 << b), 2) for b in range(bits)]
+    states = [[(jnp.int32(row), size, row)] for _, row, size, _ in streams]
 
     def plan(s, t):
-        b = orders[s][t]
-        half = total >> (t + 1)
-        bit = lax.rem(me // (1 << b), 2)
-        off = offs[s][t]
-        keep = pl.multiple_of(off + bit * half, 8)
-        send = pl.multiple_of(off + (1 - bit) * half, 8)
-        return half, keep, send, me + (1 - 2 * bit) * (1 << b)
+        lanes, _, _, order = streams[s]
+        off, size, slot = states[s][t]
+        group = order[t]
+        part = size >> len(group)
+        peers = []
+        for m in range(1 << len(group)):
+            place, device = 0, me
+            for j, b in enumerate(group):
+                flip = (m >> j) & 1
+                place = place + (1 - digit[b] if flip else digit[b]) * (1 << j)
+                device = device + flip * (1 - 2 * digit[b]) * (1 << b)
+            peers.append((pl.multiple_of(off + place * part, 8), device))
+        return lanes, part, slot, peers
 
     def start_reduce(s, t):
-        half, keep, send, partner = plan(s, t)
-        copy = pltpu.make_async_remote_copy(
-            src_ref=acc.at[s, pl.ds(send, half)], dst_ref=levels[t].at[s], send_sem=red_s.at[s, t],
-            recv_sem=red_r.at[s, t], device_id={"gx": partner}, device_id_type=MESH)
-        copy.start()
-        offs[s].append(keep)
-        return copy, half, keep
+        lanes, part, slot, peers = plan(s, t)
+        copies = []
+        for m in range(1, len(peers)):
+            region, device = peers[m]
+            copy = pltpu.make_async_remote_copy(
+                src_ref=acc.at[lanes, pl.ds(region, part)],
+                dst_ref=inbox.at[lanes, pl.ds(slot + (m - 1) * part, part)],
+                send_sem=red_s.at[s, t, m - 1], recv_sem=red_r.at[s, t, m - 1],
+                device_id={"gx": device}, device_id_type=MESH)
+            copy.start()
+            copies.append(copy)
+        states[s].append((peers[0][0], part, slot + (len(peers) - 1) * part))
+        return copies
 
     def start_gather(s, t):
-        half, keep, _, partner = plan(s, t)
-        copy = pltpu.make_async_remote_copy(
-            src_ref=whole.at[s, pl.ds(keep, half)], dst_ref=whole.at[s, pl.ds(keep, half)],
-            send_sem=red_s.at[s, bits + t], recv_sem=red_r.at[s, bits + t],
-            device_id={"gx": partner}, device_id_type=MESH)
-        copy.start()
-        return copy
-
-    flying = [start_reduce(s, 0) for s in range(2)]
-    for t in range(bits):
-        for s in range(2):
-            copy, half, keep = flying[s]
-            copy.wait()
-            reduced = acc[s, pl.ds(keep, half), :] + levels[t][s]
-            if t + 1 < bits:
-                acc[s, pl.ds(keep, half), :] = reduced
+        lanes, part, _, peers = plan(s, t)
+        kept = whole.at[lanes, pl.ds(peers[0][0], part)]
+        copies = []
+        for m in range(1, len(peers)):
+            copy = pltpu.make_async_remote_copy(
+                src_ref=kept, dst_ref=kept,
+                send_sem=red_s.at[s, stages + t, m - 1], recv_sem=red_r.at[s, stages + t, m - 1],
+                device_id={"gx": peers[m][1]}, device_id_type=MESH)
+            copy.start()
+            copies.append(copy)
+        return copies
+
+    flying = [start_reduce(s, 0) for s in range(len(streams))]
+    for t in range(stages):
+        for s in range(len(streams)):
+            lanes, part, slot, peers = plan(s, t)
+            for copy in flying[s]:
+                copy.wait()
+            reduced = acc[lanes, pl.ds(peers[0][0], part), :]
+            for m in range(len(peers) - 1):
+                reduced = reduced + inbox[lanes, slot + m * part:slot + (m + 1) * part, :]
+            if t + 1 < stages:
+                acc[lanes, pl.ds(peers[0][0], part), :] = reduced
                 flying[s] = start_reduce(s, t + 1)
             else:
-                whole[s, pl.ds(keep, half), :] = reduced
+                whole[lanes, pl.ds(peers[0][0], part), :] = reduced
                 flying[s] = start_gather(s, t)
-    for t in range(bits - 1, -1, -1):
-        for s in range(2):
-            flying[s].wait()
+    for t in range(stages - 1, -1, -1):
+        for s in range(len(streams)):
+            for copy in flying[s]:
+                copy.wait()
             if t > 0:
                 flying[s] = start_gather(s, t - 1)
     sums_out[...] = whole[...]
 
 
 def output_kernel(grad, sums, state_grad, dw_in, db_in, dw_mid, db_mid, dw_out, db_out):
-    ne, hid, nz = dw_in.shape
-    r_mid, r_out = hid, hid + ne * hid
+    ne, nz, hid = dw_in.shape
+    r_mid, r_out = ne * nz, ne * nz + ne * hid
     r_b = r_out + ne * nz
     for i in range(grad.shape[0]):
         state_grad[:, i, :] = grad[i]
     per = 128 // nz
     for e in range(ne):
         s, at = e // per, (e % per) * nz
-        dw_in[e] = sums[s, 0:hid, at:at + nz]
         db_out[e:e + 1, :] = sums[s, r_b + 32:r_b + 33, at:at + nz]
         for s in range(2):
             lanes = slice(s * 128, (s + 1) * 128)
+            dw_in[e, :, lanes] = sums[s, e * nz:(e + 1) * nz, :]
             dw_mid[e, :, lanes] = sums[s, r_mid + e * hid:r_mid + (e + 1) * hid, :]
             dw_out[e, :, lanes] = sums[s, r_out + e * nz:r_out + (e + 1) * nz, :]
     for s in range(2):
@@ -313,18 +355,21 @@
     ne, hid, _ = w_in.shape
     n = lax.axis_size("gx")
     bits = n.bit_length() - 1
-    rows = hid + ne * hid + ne * nz + 8 * n
-    bias = jnp.concatenate([b_in, b_mid, b_out], axis=1).T
-    drift_row = jnp.pad(drift[None], ((0, 0), (0, 128 - nz)))
+    rows = ne * nz + ne * hid + ne * nz + 8 * n
+    operands = (state, cotangent, kappa, labels, drift[None], jnp.transpose(w_in, (0, 2, 1)), w_mid, w_out,
+                b_in, b_mid, b_out)
     chunks, width = nx // rows_per_chunk, rows_per_chunk * ny
     vmem = pl.BlockSpec(memory_space=pltpu.VMEM)
     sds = jax.ShapeDtypeStruct
     grad, sums = pl.pallas_call(
         functools.partial(main_kernel, n),
         out_shape=(sds((nx, nz, ny), f32), sds((2, rows, 128), f32)),
-        in_specs=[vmem] * 9,
+        in_specs=[pl.BlockSpec(memory_space=pltpu.HBM)] * len(operands),
         out_specs=(vmem, vmem),
-        scratch_shapes=[
+        scratch_shapes=[pltpu.VMEM(x.shape, x.dtype) for x in operands]
+        + [
+            pltpu.SemaphoreType.DMA((len(operands),)),
+            pltpu.VMEM((2 * hid + nz, 8), f32),
             pltpu.VMEM((hid, ne * nz), bf16),
             pltpu.VMEM((ne * nz, hid), bf16),
             pltpu.VMEM((hid, ne * hid), bf16),
@@ -342,32 +387,33 @@
             pltpu.VMEM((2, 8, 128), f32),
             pltpu.VMEM((2, n, 8, 128), f32),
         ]
-        + [pltpu.VMEM((2, rows >> (t + 1), 128), f32) for t in range(bits)]
         + [
+            pltpu.VMEM((2, rows, 128), f32),
             pltpu.SemaphoreType.DMA((2,)),
             pltpu.SemaphoreType.DMA((2,)),
             pltpu.SemaphoreType.DMA((2,)),
             pltpu.SemaphoreType.DMA((2,)),
             pltpu.SemaphoreType.DMA((2, n)),
             pltpu.SemaphoreType.DMA((2, n)),
-            pltpu.SemaphoreType.DMA((2, 2 * bits)),
-            pltpu.SemaphoreType.DMA((2, 2 * bits)),
+            pltpu.SemaphoreType.DMA((4, 2 * bits, 3)),
+            pltpu.SemaphoreType.DMA((4, 2 * bits, 3)),
             pltpu.VMEM((2, rows, 128), f32),
         ],
         compiler_params=pltpu.CompilerParams(
-            collective_id=0, has_side_effects=True, vmem_limit_bytes=48 * 1024 * 1024),
+            collective_id=0, has_side_effects=True, vmem_limit_bytes=62 * 1024 * 1024),
         name="heun_reverse",
-    )(state, cotangent, kappa, labels, drift_row, w_in, w_mid, w_out, bias)
-    return tuple(pl.pallas_call(
+    )(*operands)
+    outs = pl.pallas_call(
         output_kernel,
         out_shape=(
-            sds((nz, nx, ny), f32), sds((ne, hid, nz), f32), sds((ne, hid), f32),
+            sds((nz, nx, ny), f32), sds((ne, nz, hid), f32), sds((ne, hid), f32),
             sds((ne, hid, hid), f32), sds((ne, hid), f32), sds((ne, nz, hid), f32), sds((ne, nz), f32)),
         in_specs=[vmem] * 2,
         out_specs=(vmem,) * 7,
         compiler_params=pltpu.CompilerParams(vmem_limit_bytes=32 * 1024 * 1024),
         name="place_outputs",
-    )(grad, sums))
+    )(grad, sums)
+    return (outs[0], jnp.transpose(outs[1], (0, 2, 1))) + tuple(outs[2:])
 
 
 def solution(mesh):

time: 85 us -> 69.5 us (0.82)
  Pallas kernels: 75 us -> 66.1 us
  local copies, waits for them, and re-layouts: 8.2 us -> 2.49 us
    pallas_call x1, Pallas kernels: 73.3 us -> 64.8 us  [shards(): pl.pallas_call(functools.partial(main_kernel, n), out_shape=(sds((nx, nz,...]
    unnamed x13 -> x4, local copies, waits for them, and re-layouts: 6.49 us -> 2.49 us
    pallas_call x1 -> x0, local copies, waits for them, and re-layouts: 0.89 us -> none  [shards(): pl.pallas_call(output_kernel, out_shape=(sds((nz, nx, ny), f32), sds((ne,...]
where the time goes in v2:
time: 69.5 us; the launch traced here: 69.3 us
  Pallas kernels  66.1 us (95%)
  local copies, waits for them, and re-layouts  2.49 us (4%)
    pallas_call x1, Pallas kernels, shards(): pl.pallas_call(functools.partial(main_kernel, n), out_shape=(sds((nx, nz,...  64.8 us
    unnamed x4, local copies, waits for them, and re-layouts  2.49 us

profile of v2, /device:TPU:0, one launch (start us, length us, event | category | flops | bytes accessed | tf_op | source)
XLA Modules:
  0.0 69.3 jit_solution(18101840407772636220)
XLA Ops:
  0.6 64.8 %heun_reverse.1 = (f32[16,64,128]{2,1,0:T(8,128)}, f32[2,1664,128]{2,1,0:T(8,128)}) custom-call(f32[64,16,128]{2,1,0:T(8,128)} %state_h.1, f32[64,16,128]{2,1,0:T(8,128)} %cot_h.1, f32[16,128]{1,0:T(8,128)} %kappa_h.1, s32[16,128]{1,0:T(8,128)} %labels_h.1, f32[1,64]{1,0:T(1,128)} %bitcast.4, bf16[4,64,256]{2,1,0:T(8,128)(2,1)} %bitcast.3, ...), custom_call_target="tpu_custom_call" | custom-call | tf_op jit(solution)/shard_map/heun_reverse/pallas_call | solution.py:364
  65.4 0.0 copy-start
  65.4 1.4 %copy-done = f32[2,1664,128]{2,1,0:T(8,128)S(1)} copy-done((f32[2,1664,128]{2,1,0:T(8,128)S(1)}, f32[2,1664,128]{2,1,0:T(8,128)}, u32[]{:S(2)}) %copy-start) | copy-done | bytes 1703960
  66.9 0.0 copy-start.1
  66.9 1.0 %copy-done.1 = f32[16,64,128]{2,1,0:T(8,128)S(1)} copy-done((f32[16,64,128]{2,1,0:T(8,128)S(1)}, f32[16,64,128]{2,1,0:T(8,128)}, u32[]{:S(2)}) %copy-start.1) | copy-done | bytes 524312
  67.9 1.4 %place_outputs.1 = (f32[64,16,128]{2,1,0:T(8,128)}, f32[4,64,256]{2,1,0:T(8,128)}, f32[4,256]{1,0:T(4,128)}, f32[4,256,256]{2,1,0:T(8,128)}, f32[4,256]{1,0:T(4,...) custom-call(f32[16,64,128]{2,1,0:T(8,128)S(1)} %copy-done.1, f32[2,1664,128]{2,1,0:T(8,128)S(1)} %copy-done), custom_call_target="tpu_custom_call" | custom-call | tf_op jit(solution)/shard_map/place_outputs/pallas_call | solution.py:406
Async XLA Ops:
  65.4 1.5 %copy-start = (f32[2,1664,128]{2,1,0:T(8,128)S(1)}, f32[2,1664,128]{2,1,0:T(8,128)}, u32[]{:S(2)}) copy-start(f32[2,1664,128]{2,1,0:T(8,128)} %get-tuple-element.17.sums) | copy-start | bytes 5111812
  66.9 1.0 %copy-start.1 = (f32[16,64,128]{2,1,0:T(8,128)S(1)}, f32[16,64,128]{2,1,0:T(8,128)}, u32[]{:S(2)}) copy-start(f32[16,64,128]{2,1,0:T(8,128)} %get-tuple-element.16.grad) | copy-start | bytes 1572868

commit v3 on v2

--- a/solution.py
+++ b/solution.py
@@ -59,7 +59,7 @@
     overall = nx * ny * n
     me = lax.axis_index("gx")
     right, left = lax.rem(me + 1, n), lax.rem(me + n - 1, n)
-    r_in, r_mid, r_out = 0, ne * nz, ne * nz + ne * hid
+    r_in, r_mid, r_out = 0, ne * nz + 16, ne * nz + 16 + ne * hid
     r_b = r_out + ne * nz
 
     barrier = pltpu.get_barrier_semaphore()
@@ -143,7 +143,7 @@
         acc[0, row:row + rows, :] += val[:, 0:128]
         acc[1, row:row + rows, :] += val[:, 128:256]
 
-    def backward(lab, p, hbm, z1, s1, z2, s2):
+    def backward(lab, p, hbm, z1, s1, z2, s2, ready=None):
         hot = jnp.where(lax.broadcasted_iota(jnp.int32, (16, width), 0) == lab, 1.0, 0.0).astype(bf16)
         gy = masked(lab, p.astype(bf16))
         add(r_out, dot_nt(gy, z2))
@@ -152,9 +152,11 @@
         gab2m = masked(lab, gab2)
         add(r_mid, dot_nt(gab2m, z1))
         add(r_b + 16, dot_nt(hot, gab2))
+        if ready is not None:
+            ready()
         gab1 = (dot(wmt[...], gab2m) * s1).astype(bf16)
         add(r_in, dot_nt(hbm, gab1))
-        add(r_b, dot_nt(hot, gab1))
+        add(ne * nz, dot_nt(hot, gab1))
         cols = dot(wit[...], gab1)
         return pick(lab, [cols[e * nz:(e + 1) * nz] for e in range(ne)])
 
@@ -238,17 +240,14 @@
     for copy in second_halo:
         copy.wait()
 
-    def third(c, carry):
+    def third(c, ready=None):
         lab = lab_of(c)
         hbm = masked(lab, rowcat(field, c, 0).astype(bf16))
         p = rowcat(adj, c, 0) - early_mean
-        cols = backward(lab, p, hbm, z1s[c], s1s[c], z2s[c], s2s[c])
+        cols = backward(lab, p, hbm, z1s[c], s1s[c], z2s[c], s2s[c], ready)
         for r in range(nr):
             i = c * nr + r
             grad_out[i] = base[i] + adjoint(adj, i, 0, nz) + cols[:, r * ny:(r + 1) * ny]
-        return carry
-
-    lax.fori_loop(0, chunks, third, 0)
 
     bits = n.bit_length() - 1
     units = acc.shape[1] // (8 * n)
@@ -305,9 +304,21 @@
             copies.append(copy)
         return copies
 
-    flying = [start_reduce(s, 0) for s in range(len(streams))]
+    flying = {}
+
+    def begin_high():
+        for s in (2, 3):
+            flying[s] = start_reduce(s, 0)
+
+    early_start = low >= ne * nz + 16
+    for c in range(chunks):
+        third(c, begin_high if early_start and c == chunks - 1 else None)
+    if not early_start:
+        begin_high()
+    for s in (0, 1):
+        flying[s] = start_reduce(s, 0)
     for t in range(stages):
-        for s in range(len(streams)):
+        for s in (2, 3, 0, 1):
             lanes, part, slot, peers = plan(s, t)
             for copy in flying[s]:
                 copy.wait()
@@ -321,7 +332,7 @@
                 whole[lanes, pl.ds(peers[0][0], part), :] = reduced
                 flying[s] = start_gather(s, t)
     for t in range(stages - 1, -1, -1):
-        for s in range(len(streams)):
+        for s in (2, 3, 0, 1):
             for copy in flying[s]:
                 copy.wait()
             if t > 0:
@@ -329,12 +340,17 @@
     sums_out[...] = whole[...]
 
 
-def output_kernel(grad, sums, state_grad, dw_in, db_in, dw_mid, db_mid, dw_out, db_out):
+def output_kernel(grad_h, sums_h, state_grad, dw_in, db_in, dw_mid, db_mid, dw_out, db_out, grad, sums, load):
+    loads = [pltpu.make_async_copy(sums_h, sums, load.at[0]), pltpu.make_async_copy(grad_h, grad, load.at[1])]
+    for copy in loads:
+        copy.start()
     ne, nz, hid = dw_in.shape
-    r_mid, r_out = ne * nz, ne * nz + ne * hid
+    r_mid, r_out = ne * nz + 16, ne * nz + 16 + ne * hid
     r_b = r_out + ne * nz
+    loads[1].wait()
     for i in range(grad.shape[0]):
         state_grad[:, i, :] = grad[i]
+    loads[0].wait()
     per = 128 // nz
     for e in range(ne):
         s, at = e // per, (e % per) * nz
@@ -346,7 +362,7 @@
             dw_out[e, :, lanes] = sums[s, r_out + e * nz:r_out + (e + 1) * nz, :]
     for s in range(2):
         lanes = slice(s * 128, (s + 1) * 128)
-        db_in[:, lanes] = sums[s, r_b:r_b + ne, :]
+        db_in[:, lanes] = sums[s, ne * nz:ne * nz + ne, :]
         db_mid[:, lanes] = sums[s, r_b + 16:r_b + 16 + ne, :]
 
 
@@ -408,9 +424,11 @@
         out_shape=(
             sds((nz, nx, ny), f32), sds((ne, nz, hid), f32), sds((ne, hid), f32),
             sds((ne, hid, hid), f32), sds((ne, hid), f32), sds((ne, nz, hid), f32), sds((ne, nz), f32)),
-        in_specs=[vmem] * 2,
+        in_specs=[pl.BlockSpec(memory_space=pltpu.HBM)] * 2,
         out_specs=(vmem,) * 7,
-        compiler_params=pltpu.CompilerParams(vmem_limit_bytes=32 * 1024 * 1024),
+        scratch_shapes=[pltpu.VMEM(grad.shape, f32), pltpu.VMEM(sums.shape, f32),
+                        pltpu.SemaphoreType.DMA((2,))],
+        compiler_params=pltpu.CompilerParams(vmem_limit_bytes=62 * 1024 * 1024),
         name="place_outputs",
     )(grad, sums)
     return (outs[0], jnp.transpose(outs[1], (0, 2, 1))) + tuple(outs[2:])

time: 69.5 us -> 68.3 us (0.983)
  local copies, waits for them, and re-layouts: 2.49 us -> 0 us
  Pallas kernels: 66.1 us -> 67.3 us
    unnamed x4 -> x0, local copies, waits for them, and re-layouts: 2.49 us -> none
    pallas_call x1, Pallas kernels: 1.36 us -> 3.21 us  [shards(): pl.pallas_call(output_kernel, out_shape=(sds((nz, nx, ny), f32), sds((ne,...]
where the time goes in v3:
time: 68.3 us; the launch traced here: 68.1 us
  Pallas kernels  67.3 us (99%)
  between operations  0.81 us (1%)
    pallas_call x1, Pallas kernels, shards(): pl.pallas_call(functools.partial(main_kernel, n), out_shape=(sds((nx, nz,...  64.1 us
    pallas_call x1, Pallas kernels, shards(): pl.pallas_call(output_kernel, out_shape=(sds((nz, nx, ny), f32), sds((ne,...  3.21 us

profile of v3, /device:TPU:0, one launch (start us, length us, event | category | flops | bytes accessed | tf_op | source)
XLA Modules:
  0.0 68.1 jit_solution(18308812144915357339)
XLA Ops:
  0.6 64.1 %heun_reverse.1 = (f32[16,64,128]{2,1,0:T(8,128)}, f32[2,1664,128]{2,1,0:T(8,128)}) custom-call(f32[64,16,128]{2,1,0:T(8,128)} %state_h.1, f32[64,16,128]{2,1,0:T(8,128)} %cot_h.1, f32[16,128]{1,0:T(8,128)} %kappa_h.1, s32[16,128]{1,0:T(8,128)} %labels_h.1, f32[1,64]{1,0:T(1,128)} %bitcast.4, bf16[4,64,256]{2,1,0:T(8,128)(2,1)} %bitcast.3, ...), custom_call_target="tpu_custom_call" | custom-call | tf_op jit(solution)/shard_map/heun_reverse/pallas_call | solution.py:380
  64.7 3.2 %place_outputs.1 = (f32[64,16,128]{2,1,0:T(8,128)}, f32[4,64,256]{2,1,0:T(8,128)}, f32[4,256]{1,0:T(4,128)}, f32[4,256,256]{2,1,0:T(8,128)}, f32[4,256]{1,0:T(4,...) custom-call(f32[16,64,128]{2,1,0:T(8,128)} %get-tuple-element.16.grad_h, f32[2,1664,128]{2,1,0:T(8,128)} %get-tuple-element.17.sums_h), custom_call_target="tpu_custom_call" | custom-call | tf_op jit(solution)/shard_map/place_outputs/pallas_call | solution.py:422
